TPU v7x, 32 devices: a whole 2x2x4 slice. The times are simulated.
32 devices in a mesh: tile: 8 (over y, x, core), head: 4 (over z).
Axes of the slice: x: 2, y: 2, z: 4, core: 2. Of those that a mesh axis runs over, the one named last changes fastest.
Arguments:
- bott: bfloat16 [16, 128, 1024], P('tile', 'head'), may hold values from -10 to 10
- norm_gain: float32 [1024], replicated, may hold values from 0.1 to 1.9
- w_qkv: bfloat16 [3, 1024, 1024], P(None, None, 'head'), may hold values from -1 to 1
- w_out: bfloat16 [1024, 1024], P('head'), may hold values from -3 to 3
- dw_weight: float32 [3, 3, 1024], replicated, may hold values from -2 to 2
- join_bias: float32 [1024], replicated, may hold values from -3 to 3
- w_join: bfloat16 [1024, 1024], replicated, may hold values from -0.1875 to 0.1875
Outputs:
- joined: bfloat16 [16, 128, 1024], P('tile', 'head')
All inputs are finite; a program needn't handle non-finite values.
Results may differ from a plain program's by a relative error of at most 0.02.
Values may be sent and summed in bfloat16 or wider, within the bound.
A program may use at most 128 MiB of HBM per device.

v0:
```python
import math
import jax
import jax.numpy as jnp
from jax import lax
from jax.sharding import PartitionSpec as P

HEADS = 16


def with_halo(x, sides, width):
    for axis, dim in sides:
        size, length = (lax.axis_size(axis), x.shape[dim])
        up = [(i, (i + 1) % size) for i in range(size - 1)]
        down = [(j, i) for i, j in up]
        last = lax.slice_in_dim(x, length - width, length, axis=dim)
        leading = lax.slice_in_dim(x, 0, width, axis=dim)
        before = lax.ppermute(last, axis, up)
        after = lax.ppermute(leading, axis, down)
        x = jnp.concatenate([before, x, after], axis=dim)
    return x


def fold_blocks(state, queries, key_piece, value_piece, scale):
    count, heads_here, head_dim = key_piece.shape
    block = math.gcd(count, 2048)
    key_blocks = key_piece.reshape(count // block, block, heads_here, head_dim)
    value_blocks = value_piece.reshape(count // block, block, heads_here, head_dim)

    def one_block(inner, pair):
        maxes, totals, summed = inner
        key_block, value_block = pair
        scores = (
            jnp.einsum("qhe,khe->hqk", queries, key_block, preferred_element_type=jnp.float32)
            * scale
        )
        new_max = jnp.maximum(maxes, jnp.max(scores, axis=-1))
        weights = jnp.exp(scores - new_max[..., None])
        decay = jnp.exp(maxes - new_max)
        totals = totals * decay + jnp.sum(weights, axis=-1)
        summed = summed * decay[..., None] + jnp.einsum(
            "hqk,khe->hqe",
            weights.astype(jnp.bfloat16),
            value_block,
            preferred_element_type=jnp.float32,
        )
        return ((new_max, totals, summed), None)

    return lax.scan(one_block, state, (key_blocks, value_blocks))[0]


def empty_state(heads_here, query_count, head_dim):
    return (
        jnp.full((heads_here, query_count), -1e30, jnp.float32),
        jnp.zeros((heads_here, query_count), jnp.float32),
        jnp.zeros((heads_here, query_count, head_dim), jnp.float32),
    )


def per_device(bott, norm_gain, w_qkv, w_out, dw_weight, join_bias, w_join):
    rows, cols_dev, width = bott.shape
    values = bott.astype(jnp.float32)
    normed = (
        values * lax.rsqrt(jnp.mean(values * values, axis=-1, keepdims=True) + 1e-06) * norm_gain
    ).astype(jnp.bfloat16)
    gathered = lax.all_gather(normed, "head", axis=1, tiled=True)
    columns = gathered.shape[1]
    local_width = w_qkv.shape[2]
    head_dim = width // HEADS
    local_heads = local_width // head_dim
    seq_local = columns * rows
    scale = 1.0 / head_dim**0.5
    tokens = jnp.transpose(gathered, (1, 0, 2)).reshape(seq_local, width)
    projected = jnp.einsum("td,jde->jte", tokens, w_qkv, preferred_element_type=jnp.float32).astype(
        jnp.bfloat16
    )
    queries = projected[0].reshape(seq_local, local_heads, head_dim)
    keys = projected[1]
    vals = projected[2]
    start_state = empty_state(local_heads, seq_local, head_dim)
    key_piece = lax.all_gather(keys, "tile", axis=0, tiled=True)
    value_piece = lax.all_gather(vals, "tile", axis=0, tiled=True)
    count = key_piece.shape[0]
    maxes, totals, summed = fold_blocks(
        start_state,
        queries,
        key_piece.reshape(count, local_heads, head_dim),
        value_piece.reshape(count, local_heads, head_dim),
        scale,
    )
    attended = (summed / totals[..., None]).astype(jnp.bfloat16)
    attended = jnp.transpose(attended, (1, 0, 2)).reshape(columns, rows, local_width)
    mixed = lax.psum_scatter(
        jnp.einsum("crh,hd->crd", attended, w_out, preferred_element_type=jnp.float32).astype(
            jnp.bfloat16
        ),
        "head",
        scatter_dimension=0,
        tiled=True,
    ).astype(jnp.float32)
    context = (values + jnp.transpose(mixed, (1, 0, 2))).astype(jnp.bfloat16)
    padded = with_halo(context, (("tile", 0), ("head", 1)), 1).astype(jnp.float32)
    conv = jnp.zeros((rows, cols_dev, width), jnp.float32)
    for i in range(3):
        for j in range(3):
            conv = conv + padded[i : i + rows, j : j + cols_dev] * dw_weight[i, j]
    hidden = jax.nn.gelu(conv + join_bias).astype(jnp.bfloat16)
    projected_out = jnp.einsum("rcd,de->rce", hidden, w_join, preferred_element_type=jnp.float32)
    return (context.astype(jnp.float32) + projected_out).astype(jnp.bfloat16)


def solution(mesh):
    placed = (P("tile", "head", None), P(), P(None, None, "head"), P("head", None), P(), P(), P())
    return jax.shard_map(
        per_device, mesh=mesh, in_specs=placed, out_specs=P("tile", "head", None), check_vma=False
    )
```

profile of v0, /device:TPU:11, one launch (start us, length us, event | category | flops | bytes accessed | tf_op | source)
XLA Modules:
  0.0 132.8 jit_solution(16049080055621691610)
XLA Ops:
  6.5 0.0 copy-start
  6.5 0.0 all-gather.5.cloned.1.call-start
  6.5 1.2 fusion.26
  7.7 1.0 fusion.28
  8.7 12.7 %all_gather.9 = bf16[2,128,1024]{2,1,0:T(8,128)(2,1)S(1)} all-gather(bf16[2,32,1024]{2,1,0:T(8,128)(2,1)S(1)} %fusion.28), channel_id=1, replica_groups=mesh['tile'=8,'head'=4] {'head'}, dimensions={1}, use_global_device_ids=true | all-gather | bytes 655360 | tf_op jit(solution)/shard_map/all_gather | solution.py:65
  21.4 0.5 copy.11
  21.9 0.2 reshape.37
  22.1 2.1 %fusion.6 = bf16[3,256,256]{1,2,0:T(8,128)(2,1)S(1)} fusion(bf16[256,1024,1]{1,0,2:T(8,128)(2,1)S(1)} %reshape.37, bf16[3,1024,256]{2,1,0:T(8,128)(2,1)} %param.9), kind=kOutput, calls=%fused_computation.9 | convolution fusion | flops 402849792 | bytes 2490368 | tf_op jit(solution)/shard_map/td,jde->jte/dot_general | solution.py:73
  24.3 0.7 fusion.68
  25.0 0.0 all-gather.5.cloned.1.call-update
  25.0 0.0 all-gather.7.cloned.1.call-start
  25.1 0.7 all-gather.7.cloned.1.call-update
  25.8 0.0 reduce-scatter.2.cloned.1.call-start
  25.8 28.3 %all-gather.5.cloned.1.call-done = bf16[1,2048,256]{1,2,0:T(8,128)(2,1)} async-done(((bf16[1,256,256]{1,2,0:T(8,128)(2,1)}), bf16[1,2048,256]{1,2,0:T(8,128)(2,1)}) %all-gather.5.cloned.1.call-update) | async-done | bytes 1048592 | tf_op jit(solution)/shard_map/all_gather | solution.py:80
  54.1 2.6 %multiply_reduce_fusion = (f32[4,256]{1,0:T(4,128)S(1)}, f32[4,256,2048]{2,1,0:T(8,128)S(1)}) fusion(bf16[256,4,64]{0,2,1:T(8,128)(2,1)S(1)} %bitcast.48, bf16[2048,4,64]{0,2,1:T(8,128)(2,1)} %bitcast.47), kind=kOutput, calls=%fused_computation.1 | convolution fusion | flops 272628736 | bytes 9572352 | tf_op jit(solution)/shard_map/while/body/eval_jaxpr/qhe,khe->hqk/dot_general | solution.py:33
  56.7 0.0 copy-start.1
  56.7 3.2 %copy-done.1 = f32[4,256,2048]{2,1,0:T(8,128)} copy-done((f32[4,256,2048]{2,1,0:T(8,128)}, f32[4,256,2048]{2,1,0:T(8,128)S(1)}, u32[]{:S(2)}) %copy-start.1) | copy-done | bytes 8388632
  59.9 0.0 copy-start.3
  59.9 1.6 %fusion = f32[4,256]{1,0:T(4,128)S(1)} fusion(f32[4,256,2048]{2,1,0:T(8,128)S(1)} %get-tuple-element.45, f32[4,256]{1,0:T(4,128)S(1)} %get-tuple-element.43), kind=kLoop, calls=%fused_computation.2 | loop fusion | flops 6290432 | bytes 8396800 | tf_op jit(solution)/shard_map/while/body/eval_jaxpr/reduce_sum | solution.py:39
  61.5 0.0 copy-start.2
  61.5 0.0 copy-start.4
  61.6 0.0 copy-start.5
  61.6 18.0 %all-gather.7.cloned.1.call-done = bf16[1,2048,256]{1,2,0:T(8,128)(2,1)} async-done(((bf16[1,256,256]{1,2,0:T(8,128)(2,1)}), bf16[1,2048,256]{1,2,0:T(8,128)(2,1)}) %all-gather.7.cloned.1.call-update) | async-done | bytes 1048592 | tf_op jit(solution)/shard_map/all_gather | solution.py:81
  79.6 5.2 %fusion.22 = bf16[256,4,64]{0,2,1:T(8,128)(2,1)S(1)} fusion(bf16[2048,4,64]{0,2,1:T(8,128)(2,1)} %bitcast.58, f32[4,256,2048]{2,1,0:T(8,128)} %copy-done.1, f32[4,256]{1,0:T(4,128)S(1)} %get-tuple-element.43, f32[256,4]{0,1:T(4,128)S(1)} %bitcast_add_fusion, f32[256,4]{0,1:T(4,128)S(1)} %get-tuple-element.42), kind=kOutput, calls=%fused_computation.15 | convolution fusion | flops 274923520 | bytes 9580544 | tf_op jit(solution)/shard_map/while/body/eval_jaxpr/hqk,khe->hqe/dot_general | solution.py:40
  84.8 0.2 copy.13
  85.0 0.2 reshape.32
  85.2 0.0 copy-done.3
  85.2 1.1 convolution_convert_fusion
  86.3 0.0 reduce-scatter.2.cloned.1.call-update
  86.3 17.5 %reduce-scatter.2.cloned.1.call-done = bf16[32,2,1024]{2,0,1:T(8,128)(2,1)} async-done(((bf16[128,2,1024]{2,0,1:T(8,128)(2,1)}), bf16[32,2,1024]{2,0,1:T(8,128)(2,1)}) %reduce-scatter.2.cloned.1.call-update) | async-done | bytes 131088 | tf_op jit(solution)/shard_map/reduce_scatter | solution.py:92
  103.8 0.0 copy-done.2
  103.8 0.9 fusion.29
  104.8 4.4 %collective-permute-start = (bf16[1,32,1024]{2,1,0:T(8,128)(2,1)S(1)}, bf16[1,32,1024]{2,1,0:T(8,128)(2,1)S(1)}, u32[]{:S(2)}, u32[]{:S(2)}) collective-permute-start(bf16[1,32,1024]{2,1,0:T(8,128)(2,1)S(1)} %get-tuple-element.30), channel_id=1, source_target_pairs={{0,4},{4,8},{8,12},{12,16},{16,20},{20,24},{24,28},{1,5},{5,9},{9,... | collective-permute-start | bytes 196616 | tf_op jit(solution)/shard_map/ppermute | solution.py:17
  109.2 1.9 %collective-permute-start.1 = (bf16[1,32,1024]{2,1,0:T(8,128)(2,1)S(1)}, bf16[1,32,1024]{2,1,0:T(8,128)(2,1)S(1)}, u32[]{:S(2)}, u32[]{:S(2)}) collective-permute-start(bf16[1,32,1024]{2,1,0:T(8,128)(2,1)S(1)} %get-tuple-element.32), channel_id=1, source_target_pairs={{4,0},{8,4},{12,8},{16,12},{20,16},{24,20},{28,24},{5,1},{9,5},{13... | collective-permute-start | bytes 196616 | tf_op jit(solution)/shard_map/ppermute | solution.py:18
  111.2 0.0 collective-permute-done
  111.2 4.5 %collective-permute-done.1 = bf16[1,32,1024]{2,1,0:T(8,128)(2,1)S(1)} collective-permute-done((bf16[1,32,1024]{2,1,0:T(8,128)(2,1)S(1)}, bf16[1,32,1024]{2,1,0:T(8,128)(2,1)S(1)}, u32[]{:S(2)}, u32[]{:S(2)}) %collective-permute-start.1) | collective-permute-done | bytes 65568 | tf_op jit(solution)/shard_map/ppermute | solution.py:18
  115.8 4.5 %collective-permute-start.2 = (bf16[4,1,1024]{2,1,0:T(2,128)(2,1)S(1)}, bf16[4,1,1024]{2,1,0:T(2,128)(2,1)S(1)}, u32[]{:S(2)}, u32[]{:S(2)}) collective-permute-start(bf16[4,1,1024]{2,1,0:T(2,128)(2,1)S(1)} %get-tuple-element.20), channel_id=1, source_target_pairs={{0,1},{1,2},{2,3},{4,5},{5,6},{6,7},{8,9},{9,10},{10,11},{12,13},{... | collective-permute-start | bytes 24584 | tf_op jit(solution)/shard_map/ppermute | solution.py:17
  120.2 2.0 %collective-permute-start.3 = (bf16[4,1,1024]{2,1,0:T(2,128)(2,1)S(1)}, bf16[4,1,1024]{2,1,0:T(2,128)(2,1)S(1)}, u32[]{:S(2)}, u32[]{:S(2)}) collective-permute-start(bf16[4,1,1024]{2,1,0:T(2,128)(2,1)S(1)} %get-tuple-element.28), channel_id=1, source_target_pairs={{1,0},{2,1},{3,2},{5,4},{6,5},{7,6},{9,8},{10,9},{11,10},{13,12},{... | collective-permute-start | bytes 24584 | tf_op jit(solution)/shard_map/ppermute | solution.py:18
  122.3 0.0 copy-done.4
  122.3 0.0 collective-permute-done.2
  122.3 2.4 %collective-permute-done.3 = bf16[4,1,1024]{2,1,0:T(2,128)(2,1)S(1)} collective-permute-done((bf16[4,1,1024]{2,1,0:T(2,128)(2,1)S(1)}, bf16[4,1,1024]{2,1,0:T(2,128)(2,1)S(1)}, u32[]{:S(2)}, u32[]{:S(2)}) %collective-permute-start.3) | collective-permute-done | bytes 8224 | tf_op jit(solution)/shard_map/ppermute | solution.py:18
  124.7 0.1 maximum_convert_fusion
  124.8 0.0 copy-done
  124.8 0.0 copy-done.5
  124.9 1.4 %fusion.16 = bf16[2,32,1024]{2,1,0:T(8,128)(2,1)} fusion(bf16[1024,1024]{1,0:T(8,128)(2,1)S(1)} %copy-done, bf16[2,32,1024]{2,1,0:T(8,128)(2,1)S(1)} %fusion.29, f32[4,34,1024]{2,1,0:T(8,128)S(1)} %maximum_convert_fusion, f32[1024]{0:T(1024)S(1)} %copy-done.5, f32[1024]{0:T(1024)S(1)} %bitcast.56, f32[1024]{0:T(1024)S(1)} %bitcast.57, ...), kind=kOutput, calls=%fused_computation.13 | convolution fusion | flops 136183808 | bytes 4759552 | tf_op jit(solution)/shard_map/rcd,de->rce/dot_general | solution.py:107
  (6 shorter events, 0.1 us)
Async XLA Ops:
  6.5 118.3 %copy-start = (bf16[1024,1024]{1,0:T(8,128)(2,1)S(1)}, bf16[1024,1024]{1,0:T(8,128)(2,1)}, u32[]{:S(2)}) copy-start(bf16[1024,1024]{1,0:T(8,128)(2,1)} %param.13) | copy-start | bytes 6291460
  6.5 47.5 %all-gather.5.cloned.1.call-start = ((), (), s32[]{:S(2)}) async-start(), calls=%async_computation.2 | async-start | bytes 1179648 | tf_op jit(solution)/shard_map/all_gather | solution.py:80
  25.0 54.5 %all-gather.7.cloned.1.call-start = ((), (), s32[]{:S(2)}) async-start(), calls=%async_computation.3 | async-start | bytes 1179648 | tf_op jit(solution)/shard_map/all_gather | solution.py:81
  25.8 78.1 %reduce-scatter.2.cloned.1.call-start = ((), (), s32[]{:S(2)}) async-start(), calls=%async_computation.1 | async-start | bytes 655360 | tf_op jit(solution)/shard_map/reduce_scatter | solution.py:92
  56.7 3.2 %copy-start.1 = (f32[4,256,2048]{2,1,0:T(8,128)}, f32[4,256,2048]{2,1,0:T(8,128)S(1)}, u32[]{:S(2)}) copy-start(f32[4,256,2048]{2,1,0:T(8,128)S(1)} %get-tuple-element.45) | copy-start | bytes 25165828
  59.9 25.3 %copy-start.3 = (bf16[256,1024]{1,0:T(8,128)(2,1)S(1)}, bf16[256,1024]{1,0:T(8,128)(2,1)}, u32[]{:S(2)}) copy-start(bf16[256,1024]{1,0:T(8,128)(2,1)} %param.10) | copy-start | bytes 1572868
  61.5 42.3 %copy-start.2 = (bf16[2,32,1024]{2,1,0:T(8,128)(2,1)S(1)}, bf16[2,32,1024]{2,1,0:T(8,128)(2,1)}, u32[]{:S(2)}) copy-start(bf16[2,32,1024]{2,1,0:T(8,128)(2,1)} %param.7) | copy-start | bytes 393220
  61.5 60.7 %copy-start.4 = (f32[3,3,1024]{2,1,0:T(4,128)S(1)}, f32[3,3,1024]{2,1,0:T(4,128)}, u32[]{:S(2)}) copy-start(f32[3,3,1024]{2,1,0:T(4,128)} %param.11) | copy-start | bytes 110596
  61.6 63.3 %copy-start.5 = (f32[1024]{0:T(1024)S(1)}, f32[1024]{0:T(1024)}, u32[]{:S(2)}) copy-start(f32[1024]{0:T(1024)} %param.12) | copy-start | bytes 12292
  104.8 6.4 %collective-permute-start = (bf16[1,32,1024]{2,1,0:T(8,128)(2,1)S(1)}, bf16[1,32,1024]{2,1,0:T(8,128)(2,1)S(1)}, u32[]{:S(2)}, u32[]{:S(2)}) collective-permute-start(bf16[1,32,1024]{2,1,0:T(8,128)(2,1)S(1)} %get-tuple-element.30), channel_id=1, source_target_pairs={{0,4},{4,8},{8,12},{12,16},{16,20},{20,24},{24,28},{1,5},{5,9},{9,... | collective-permute-start | bytes 196616 | tf_op jit(solution)/shard_map/ppermute | solution.py:17
  109.2 6.5 %collective-permute-start.1 = (bf16[1,32,1024]{2,1,0:T(8,128)(2,1)S(1)}, bf16[1,32,1024]{2,1,0:T(8,128)(2,1)S(1)}, u32[]{:S(2)}, u32[]{:S(2)}) collective-permute-start(bf16[1,32,1024]{2,1,0:T(8,128)(2,1)S(1)} %get-tuple-element.32), channel_id=1, source_target_pairs={{4,0},{8,4},{12,8},{16,12},{20,16},{24,20},{28,24},{5,1},{9,5},{13... | collective-permute-start | bytes 196616 | tf_op jit(solution)/shard_map/ppermute | solution.py:18
  115.8 6.5 %collective-permute-start.2 = (bf16[4,1,1024]{2,1,0:T(2,128)(2,1)S(1)}, bf16[4,1,1024]{2,1,0:T(2,128)(2,1)S(1)}, u32[]{:S(2)}, u32[]{:S(2)}) collective-permute-start(bf16[4,1,1024]{2,1,0:T(2,128)(2,1)S(1)} %get-tuple-element.20), channel_id=1, source_target_pairs={{0,1},{1,2},{2,3},{4,5},{5,6},{6,7},{8,9},{9,10},{10,11},{12,13},{... | collective-permute-start | bytes 24584 | tf_op jit(solution)/shard_map/ppermute | solution.py:17
  120.2 4.5 %collective-permute-start.3 = (bf16[4,1,1024]{2,1,0:T(2,128)(2,1)S(1)}, bf16[4,1,1024]{2,1,0:T(2,128)(2,1)S(1)}, u32[]{:S(2)}, u32[]{:S(2)}) collective-permute-start(bf16[4,1,1024]{2,1,0:T(2,128)(2,1)S(1)} %get-tuple-element.28), channel_id=1, source_target_pairs={{1,0},{2,1},{3,2},{5,4},{6,5},{7,6},{9,8},{10,9},{11,10},{13,12},{... | collective-permute-start | bytes 24584 | tf_op jit(solution)/shard_map/ppermute | solution.py:18
Sparse Core Ops, SparseCore 0:
  25.1 28.8 all-gather.4
  56.0 23.5 all-gather.6
  86.5 17.3 reduce-scatter.1
where the time goes:
time: 133 us
  waiting for transfers between devices  71.4 us (54%)
  between operations  13.3 us (10%)
  starting transfers between devices  12.9 us (10%)
  blocking collectives  12.7 us (10%)
  matrix products  12.5 us (9%)
  local copies, waits for them, and re-layouts  5.13 us (4%)
  other arithmetic  4.91 us (4%)
    all_gather x1, waiting for transfers between devices, per_device(): key_piece = lax.all_gather(keys, 'tile', axis=0, tiled=True)  28.3 us
    all_gather x1, waiting for transfers between devices, per_device(): value_piece = lax.all_gather(vals, 'tile', axis=0, tiled=True)  18 us
    reduce_scatter x1, waiting for transfers between devices, per_device(): lax.psum_scatter(jnp.einsum('crh,hd->crd', attended, w_out, preferred_ele...  17.5 us
    all_gather x1, blocking collectives, per_device(): gathered = lax.all_gather(normed, 'head', axis=1, tiled=True)  12.7 us
    ppermute x2, starting transfers between devices, with_halo(): before = lax.ppermute(last, axis, up)  8.89 us
    ppermute x2, waiting for transfers between devices, with_halo(): after = lax.ppermute(leading, axis, down)  6.94 us
    dot_general x1, matrix products, one_block(): jnp.einsum('hqk,khe->hqe', weights.astype(jnp.bfloat16), value_block, pre...  5.24 us
    ppermute x2, starting transfers between devices, with_halo(): after = lax.ppermute(leading, axis, down)  3.95 us
  transfers between devices with their start and end apart: 7, of which 5 were waited for; matrix products, arithmetic and copies ran while one was open for 3% of the time, Pallas kernels for 0%

commit v1 on v0

--- a/solution.py
+++ b/solution.py
@@ -62,7 +62,23 @@
     normed = (
         values * lax.rsqrt(jnp.mean(values * values, axis=-1, keepdims=True) + 1e-06) * norm_gain
     ).astype(jnp.bfloat16)
-    gathered = lax.all_gather(normed, "head", axis=1, tiled=True)
+    ways, here, step = (lax.axis_size("head"), lax.axis_index("head"), normed.shape[1])
+    dims = [n * ways if d == 1 else n for d, n in enumerate(normed.shape)]
+    full = lax.dynamic_update_slice_in_dim(
+        jnp.zeros(dims, normed.dtype), normed, here * step, axis=1
+    )
+    going_up = going_down = normed
+    for far in range(1, ways // 2 + 1):
+        going_up = lax.ppermute(going_up, "head", [(d, (d + 1) % ways) for d in range(ways)])
+        full = lax.dynamic_update_slice_in_dim(full, going_up, (here - far) % ways * step, axis=1)
+        if 2 * far < ways:
+            going_down = lax.ppermute(
+                going_down, "head", [(d, (d - 1) % ways) for d in range(ways)]
+            )
+            full = lax.dynamic_update_slice_in_dim(
+                full, going_down, (here + far) % ways * step, axis=1
+            )
+    gathered = full
     columns = gathered.shape[1]
     local_width = w_qkv.shape[2]
     head_dim = width // HEADS

time: 133 us -> 129 us (0.970)
  blocking collectives: 12.7 us -> 0 us
  waiting for transfers between devices: 71.4 us -> 76.9 us
  starting transfers between devices: 12.9 us -> 15.7 us
    all_gather x1 -> x0, blocking collectives: 12.7 us -> none  [per_device(): gathered = lax.all_gather(normed, 'head', axis=1, tiled=True)]
    ppermute x0 -> x3, waiting for transfers between devices: none -> 5.94 us  [the longest x1 3.26 us: per_device(): lax.ppermute(going_down, 'head', [(d, (d - 1) % ways) for d in range(ways)])]
    ppermute x0 -> x3, starting transfers between devices: none -> 2.81 us  [the longest x2 2.65 us: per_device(): lax.ppermute(going_up, 'head', [(d, (d + 1) % ways) for d in range(ways)])]
  transfers between devices with their start and end apart: 7 -> 10, of which waited for: 5 -> 8; matrix products, arithmetic and copies ran while one was open for 3% -> 4% of each run, Pallas kernels for 0% -> 0%
where the time goes in v1:
time: 129 us
  waiting for transfers between devices  76.9 us (60%)
  starting transfers between devices  15.7 us (12%)
  between operations  13.3 us (10%)
  matrix products  12.5 us (10%)
  local copies, waits for them, and re-layouts  5.48 us (4%)
  other arithmetic  4.91 us (4%)
    all_gather x1, waiting for transfers between devices, per_device(): key_piece = lax.all_gather(keys, 'tile', axis=0, tiled=True)  27.9 us
    all_gather x1, waiting for transfers between devices, per_device(): value_piece = lax.all_gather(vals, 'tile', axis=0, tiled=True)  18 us
    reduce_scatter x1, waiting for transfers between devices, per_device(): lax.psum_scatter(jnp.einsum('crh,hd->crd', attended, w_out, preferred_ele...  17.5 us
    ppermute x2, starting transfers between devices, with_halo(): before = lax.ppermute(last, axis, up)  8.84 us
    ppermute x2, waiting for transfers between devices, with_halo(): after = lax.ppermute(leading, axis, down)  6.94 us
    dot_general x1, matrix products, one_block(): jnp.einsum('hqk,khe->hqe', weights.astype(jnp.bfloat16), value_block, pre...  5.24 us
    ppermute x2, starting transfers between devices, with_halo(): after = lax.ppermute(leading, axis, down)  3.94 us
    ppermute x1, waiting for transfers between devices, per_device(): lax.ppermute(going_down, 'head', [(d, (d - 1) % ways) for d in range(ways)])  3.26 us
  transfers between devices with their start and end apart: 10, of which 8 were waited for; matrix products, arithmetic and copies ran while one was open for 4% of the time, Pallas kernels for 0%

profile of v1, /device:TPU:11, one launch (start us, length us, event | category | flops | bytes accessed | tf_op | source)
XLA Modules:
  0.0 128.8 jit_solution(17604495608117733269)
XLA Ops:
  6.5 0.0 copy-start
  6.5 0.0 all-gather.5.cloned.1.call-start
  6.5 1.2 fusion.26
  7.7 1.0 fusion.28
  8.7 1.3 %collective-permute-start = (bf16[2,32,1024]{2,1,0:T(8,128)(2,1)S(1)}, bf16[2,32,1024]{2,1,0:T(8,128)(2,1)S(1)}, u32[]{:S(2)}, u32[]{:S(2)}) collective-permute-start(bf16[2,32,1024]{2,1,0:T(8,128)(2,1)S(1)} %fusion.28), channel_id=1, source_target_pairs={{0,1},{1,2},{2,3},{3,0},{4,5},{5,6},{6,7},{7,4},{8,9},{9,10},{10,1... | collective-permute-start | bytes 393224 | tf_op jit(solution)/shard_map/ppermute | solution.py:72
  10.1 0.2 collective-permute-start.1
  10.2 0.3 broadcast_in_dim.20
  10.5 0.2 copy_dynamic-update-slice_fusion.3
  10.7 2.5 %collective-permute-done = bf16[2,32,1024]{2,1,0:T(8,128)(2,1)S(1)} collective-permute-done((bf16[2,32,1024]{2,1,0:T(8,128)(2,1)S(1)}, bf16[2,32,1024]{2,1,0:T(8,128)(2,1)S(1)}, u32[]{:S(2)}, u32[]{:S(2)}) %collective-permute-start) | collective-permute-done | bytes 131104 | tf_op jit(solution)/shard_map/ppermute | solution.py:72
  13.1 1.3 %collective-permute-start.2 = (bf16[2,32,1024]{2,1,0:T(8,128)(2,1)S(1)}, bf16[2,32,1024]{2,1,0:T(8,128)(2,1)S(1)}, u32[]{:S(2)}, u32[]{:S(2)}) collective-permute-start(bf16[2,32,1024]{2,1,0:T(8,128)(2,1)S(1)} %collective-permute-done), channel_id=1, source_target_pairs={{0,1},{1,2},{2,3},{3,0},{4,5},{5,6},{6,7},{7,4},{8,9},{9,10},{10,1... | collective-permute-start | bytes 393224 | tf_op jit(solution)/shard_map/ppermute | solution.py:72
  14.4 0.2 copy_dynamic-update-slice_fusion.2
  14.6 3.3 %collective-permute-done.1 = bf16[2,32,1024]{2,1,0:T(8,128)(2,1)S(1)} collective-permute-done((bf16[2,32,1024]{2,1,0:T(8,128)(2,1)S(1)}, bf16[2,32,1024]{2,1,0:T(8,128)(2,1)S(1)}, u32[]{:S(2)}, u32[]{:S(2)}) %collective-permute-start.1) | collective-permute-done | bytes 131104 | tf_op jit(solution)/shard_map/ppermute | solution.py:75
  17.9 0.2 copy_dynamic-update-slice_fusion.1
  18.0 0.2 collective-permute-done.2
  18.2 0.2 copy_dynamic-update-slice_fusion
  18.4 0.2 reshape.37
  18.6 2.1 %fusion.6 = bf16[3,256,256]{1,2,0:T(8,128)(2,1)S(1)} fusion(bf16[256,1024,1]{1,0,2:T(8,128)(2,1)S(1)} %reshape.37, bf16[3,1024,256]{2,1,0:T(8,128)(2,1)} %param.9), kind=kOutput, calls=%fused_computation.9 | convolution fusion | flops 402849792 | bytes 2490368 | tf_op jit(solution)/shard_map/td,jde->jte/dot_general | solution.py:89
  20.7 0.7 fusion.68
  21.4 0.0 all-gather.5.cloned.1.call-update
  21.5 0.0 all-gather.7.cloned.1.call-start
  21.5 0.7 all-gather.7.cloned.1.call-update
  22.2 0.0 reduce-scatter.2.cloned.1.call-start
  22.3 27.9 %all-gather.5.cloned.1.call-done = bf16[1,2048,256]{1,2,0:T(8,128)(2,1)} async-done(((bf16[1,256,256]{1,2,0:T(8,128)(2,1)}), bf16[1,2048,256]{1,2,0:T(8,128)(2,1)}) %all-gather.5.cloned.1.call-update) | async-done | bytes 1048592 | tf_op jit(solution)/shard_map/all_gather | solution.py:96
  50.1 2.6 %multiply_reduce_fusion = (f32[4,256]{1,0:T(4,128)S(1)}, f32[4,256,2048]{2,1,0:T(8,128)S(1)}) fusion(bf16[256,4,64]{0,2,1:T(8,128)(2,1)S(1)} %bitcast.48, bf16[2048,4,64]{0,2,1:T(8,128)(2,1)} %bitcast.47), kind=kOutput, calls=%fused_computation.1 | convolution fusion | flops 272628736 | bytes 9572352 | tf_op jit(solution)/shard_map/while/body/eval_jaxpr/qhe,khe->hqk/dot_general | solution.py:33
  52.7 3.2 %copy-done.1 = f32[4,256,2048]{2,1,0:T(8,128)} copy-done((f32[4,256,2048]{2,1,0:T(8,128)}, f32[4,256,2048]{2,1,0:T(8,128)S(1)}, u32[]{:S(2)}) %copy-start.1) | copy-done | bytes 8388632
  55.9 1.6 %fusion = f32[4,256]{1,0:T(4,128)S(1)} fusion(f32[4,256,2048]{2,1,0:T(8,128)S(1)} %get-tuple-element.45, f32[4,256]{1,0:T(4,128)S(1)} %get-tuple-element.43), kind=kLoop, calls=%fused_computation.2 | loop fusion | flops 6290432 | bytes 8396800 | tf_op jit(solution)/shard_map/while/body/eval_jaxpr/reduce_sum | solution.py:39
  57.6 0.0 copy-start.2
  57.6 0.0 copy-start.4
  57.6 0.0 copy-start.5
  57.6 18.0 %all-gather.7.cloned.1.call-done = bf16[1,2048,256]{1,2,0:T(8,128)(2,1)} async-done(((bf16[1,256,256]{1,2,0:T(8,128)(2,1)}), bf16[1,2048,256]{1,2,0:T(8,128)(2,1)}) %all-gather.7.cloned.1.call-update) | async-done | bytes 1048592 | tf_op jit(solution)/shard_map/all_gather | solution.py:97
  75.6 5.2 %fusion.22 = bf16[256,4,64]{0,2,1:T(8,128)(2,1)S(1)} fusion(bf16[2048,4,64]{0,2,1:T(8,128)(2,1)} %bitcast.58, f32[4,256,2048]{2,1,0:T(8,128)} %copy-done.1, f32[4,256]{1,0:T(4,128)S(1)} %get-tuple-element.43, f32[256,4]{0,1:T(4,128)S(1)} %bitcast_add_fusion, f32[256,4]{0,1:T(4,128)S(1)} %get-tuple-element.42), kind=kOutput, calls=%fused_computation.15 | convolution fusion | flops 274923520 | bytes 9580544 | tf_op jit(solution)/shard_map/while/body/eval_jaxpr/hqk,khe->hqe/dot_general | solution.py:40
  80.8 0.2 copy.19
  81.0 0.2 reshape.32
  81.3 1.1 convolution_convert_fusion
  82.4 0.0 reduce-scatter.2.cloned.1.call-update
  82.4 17.5 %reduce-scatter.2.cloned.1.call-done = bf16[32,2,1024]{2,0,1:T(8,128)(2,1)} async-done(((bf16[128,2,1024]{2,0,1:T(8,128)(2,1)}), bf16[32,2,1024]{2,0,1:T(8,128)(2,1)}) %reduce-scatter.2.cloned.1.call-update) | async-done | bytes 131088 | tf_op jit(solution)/shard_map/reduce_scatter | solution.py:108
  99.9 0.9 fusion.29
  100.9 4.4 %collective-permute-start.3 = (bf16[1,32,1024]{2,1,0:T(8,128)(2,1)S(1)}, bf16[1,32,1024]{2,1,0:T(8,128)(2,1)S(1)}, u32[]{:S(2)}, u32[]{:S(2)}) collective-permute-start(bf16[1,32,1024]{2,1,0:T(8,128)(2,1)S(1)} %get-tuple-element.30), channel_id=1, source_target_pairs={{0,4},{4,8},{8,12},{12,16},{16,20},{20,24},{24,28},{1,5},{5,9},{9,... | collective-permute-start | bytes 196616 | tf_op jit(solution)/shard_map/ppermute | solution.py:17
  105.3 1.9 %collective-permute-start.4 = (bf16[1,32,1024]{2,1,0:T(8,128)(2,1)S(1)}, bf16[1,32,1024]{2,1,0:T(8,128)(2,1)S(1)}, u32[]{:S(2)}, u32[]{:S(2)}) collective-permute-start(bf16[1,32,1024]{2,1,0:T(8,128)(2,1)S(1)} %get-tuple-element.32), channel_id=1, source_target_pairs={{4,0},{8,4},{12,8},{16,12},{20,16},{24,20},{28,24},{5,1},{9,5},{13... | collective-permute-start | bytes 196616 | tf_op jit(solution)/shard_map/ppermute | solution.py:18
  107.2 0.0 collective-permute-done.3
  107.2 4.5 %collective-permute-done.4 = bf16[1,32,1024]{2,1,0:T(8,128)(2,1)S(1)} collective-permute-done((bf16[1,32,1024]{2,1,0:T(8,128)(2,1)S(1)}, bf16[1,32,1024]{2,1,0:T(8,128)(2,1)S(1)}, u32[]{:S(2)}, u32[]{:S(2)}) %collective-permute-start.4) | collective-permute-done | bytes 65568 | tf_op jit(solution)/shard_map/ppermute | solution.py:18
  111.8 4.4 %collective-permute-start.5 = (bf16[4,1,1024]{2,1,0:T(2,128)(2,1)S(1)}, bf16[4,1,1024]{2,1,0:T(2,128)(2,1)S(1)}, u32[]{:S(2)}, u32[]{:S(2)}) collective-permute-start(bf16[4,1,1024]{2,1,0:T(2,128)(2,1)S(1)} %get-tuple-element.20), channel_id=1, source_target_pairs={{0,1},{1,2},{2,3},{4,5},{5,6},{6,7},{8,9},{9,10},{10,11},{12,13},{... | collective-permute-start | bytes 24584 | tf_op jit(solution)/shard_map/ppermute | solution.py:17
  116.2 2.0 %collective-permute-start.6 = (bf16[4,1,1024]{2,1,0:T(2,128)(2,1)S(1)}, bf16[4,1,1024]{2,1,0:T(2,128)(2,1)S(1)}, u32[]{:S(2)}, u32[]{:S(2)}) collective-permute-start(bf16[4,1,1024]{2,1,0:T(2,128)(2,1)S(1)} %get-tuple-element.28), channel_id=1, source_target_pairs={{1,0},{2,1},{3,2},{5,4},{6,5},{7,6},{9,8},{10,9},{11,10},{13,12},{... | collective-permute-start | bytes 24584 | tf_op jit(solution)/shard_map/ppermute | solution.py:18
  118.3 0.0 copy-done.4
  118.3 0.0 collective-permute-done.5
  118.3 2.4 %collective-permute-done.6 = bf16[4,1,1024]{2,1,0:T(2,128)(2,1)S(1)} collective-permute-done((bf16[4,1,1024]{2,1,0:T(2,128)(2,1)S(1)}, bf16[4,1,1024]{2,1,0:T(2,128)(2,1)S(1)}, u32[]{:S(2)}, u32[]{:S(2)}) %collective-permute-start.6) | collective-permute-done | bytes 8224 | tf_op jit(solution)/shard_map/ppermute | solution.py:18
  120.7 0.1 maximum_convert_fusion
  120.9 1.4 %fusion.16 = bf16[2,32,1024]{2,1,0:T(8,128)(2,1)} fusion(bf16[1024,1024]{1,0:T(8,128)(2,1)S(1)} %copy-done, bf16[2,32,1024]{2,1,0:T(8,128)(2,1)S(1)} %fusion.29, f32[4,34,1024]{2,1,0:T(8,128)S(1)} %maximum_convert_fusion, f32[1024]{0:T(1024)S(1)} %copy-done.5, f32[1024]{0:T(1024)S(1)} %bitcast.56, f32[1024]{0:T(1024)S(1)} %bitcast.57, ...), kind=kOutput, calls=%fused_computation.13 | convolution fusion | flops 136183808 | bytes 4759552 | tf_op jit(solution)/shard_map/rcd,de->rce/dot_general | solution.py:123
  (12 shorter events, 0.1 us)
Async XLA Ops:
  6.5 114.3 %copy-start = (bf16[1024,1024]{1,0:T(8,128)(2,1)S(1)}, bf16[1024,1024]{1,0:T(8,128)(2,1)}, u32[]{:S(2)}) copy-start(bf16[1024,1024]{1,0:T(8,128)(2,1)} %param.13) | copy-start | bytes 6291460
  6.5 43.6 %all-gather.5.cloned.1.call-start = ((), (), s32[]{:S(2)}) async-start(), calls=%async_computation.2 | async-start | bytes 1179648 | tf_op jit(solution)/shard_map/all_gather | solution.py:96
  8.7 4.4 %collective-permute-start = (bf16[2,32,1024]{2,1,0:T(8,128)(2,1)S(1)}, bf16[2,32,1024]{2,1,0:T(8,128)(2,1)S(1)}, u32[]{:S(2)}, u32[]{:S(2)}) collective-permute-start(bf16[2,32,1024]{2,1,0:T(8,128)(2,1)S(1)} %fusion.28), channel_id=1, source_target_pairs={{0,1},{1,2},{2,3},{3,0},{4,5},{5,6},{6,7},{7,4},{8,9},{9,10},{10,1... | collective-permute-start | bytes 393224 | tf_op jit(solution)/shard_map/ppermute | solution.py:72
  10.1 7.8 %collective-permute-start.1 = (bf16[2,32,1024]{2,1,0:T(8,128)(2,1)S(1)}, bf16[2,32,1024]{2,1,0:T(8,128)(2,1)S(1)}, u32[]{:S(2)}, u32[]{:S(2)}) collective-permute-start(bf16[2,32,1024]{2,1,0:T(8,128)(2,1)S(1)} %fusion.28), channel_id=1, source_target_pairs={{0,3},{1,0},{2,1},{3,2},{4,7},{5,4},{6,5},{7,6},{8,11},{9,8},{10,9... | collective-permute-start | bytes 393224 | tf_op jit(solution)/shard_map/ppermute | solution.py:75
  13.1 5.1 %collective-permute-start.2 = (bf16[2,32,1024]{2,1,0:T(8,128)(2,1)S(1)}, bf16[2,32,1024]{2,1,0:T(8,128)(2,1)S(1)}, u32[]{:S(2)}, u32[]{:S(2)}) collective-permute-start(bf16[2,32,1024]{2,1,0:T(8,128)(2,1)S(1)} %collective-permute-done), channel_id=1, source_target_pairs={{0,1},{1,2},{2,3},{3,0},{4,5},{5,6},{6,7},{7,4},{8,9},{9,10},{10,1... | collective-permute-start | bytes 393224 | tf_op jit(solution)/shard_map/ppermute | solution.py:72
  21.5 54.1 %all-gather.7.cloned.1.call-start = ((), (), s32[]{:S(2)}) async-start(), calls=%async_computation.3 | async-start | bytes 1179648 | tf_op jit(solution)/shard_map/all_gather | solution.py:97
  22.2 77.7 %reduce-scatter.2.cloned.1.call-start = ((), (), s32[]{:S(2)}) async-start(), calls=%async_computation.1 | async-start | bytes 655360 | tf_op jit(solution)/shard_map/reduce_scatter | solution.py:108
  52.7 3.2 %copy-start.1 = (f32[4,256,2048]{2,1,0:T(8,128)}, f32[4,256,2048]{2,1,0:T(8,128)S(1)}, u32[]{:S(2)}) copy-start(f32[4,256,2048]{2,1,0:T(8,128)S(1)} %get-tuple-element.45) | copy-start | bytes 25165828
  55.9 25.3 %copy-start.3 = (bf16[256,1024]{1,0:T(8,128)(2,1)S(1)}, bf16[256,1024]{1,0:T(8,128)(2,1)}, u32[]{:S(2)}) copy-start(bf16[256,1024]{1,0:T(8,128)(2,1)} %param.10) | copy-start | bytes 1572868
  57.6 42.3 %copy-start.2 = (bf16[2,32,1024]{2,1,0:T(8,128)(2,1)S(1)}, bf16[2,32,1024]{2,1,0:T(8,128)(2,1)}, u32[]{:S(2)}) copy-start(bf16[2,32,1024]{2,1,0:T(8,128)(2,1)} %param.7) | copy-start | bytes 393220
  57.6 60.7 %copy-start.4 = (f32[3,3,1024]{2,1,0:T(4,128)S(1)}, f32[3,3,1024]{2,1,0:T(4,128)}, u32[]{:S(2)}) copy-start(f32[3,3,1024]{2,1,0:T(4,128)} %param.11) | copy-start | bytes 110596
  57.6 63.3 %copy-start.5 = (f32[1024]{0:T(1024)S(1)}, f32[1024]{0:T(1024)}, u32[]{:S(2)}) copy-start(f32[1024]{0:T(1024)} %param.12) | copy-start | bytes 12292
  100.9 6.3 %collective-permute-start.3 = (bf16[1,32,1024]{2,1,0:T(8,128)(2,1)S(1)}, bf16[1,32,1024]{2,1,0:T(8,128)(2,1)S(1)}, u32[]{:S(2)}, u32[]{:S(2)}) collective-permute-start(bf16[1,32,1024]{2,1,0:T(8,128)(2,1)S(1)} %get-tuple-element.30), channel_id=1, source_target_pairs={{0,4},{4,8},{8,12},{12,16},{16,20},{20,24},{24,28},{1,5},{5,9},{9,... | collective-permute-start | bytes 196616 | tf_op jit(solution)/shard_map/ppermute | solution.py:17
  105.3 6.5 %collective-permute-start.4 = (bf16[1,32,1024]{2,1,0:T(8,128)(2,1)S(1)}, bf16[1,32,1024]{2,1,0:T(8,128)(2,1)S(1)}, u32[]{:S(2)}, u32[]{:S(2)}) collective-permute-start(bf16[1,32,1024]{2,1,0:T(8,128)(2,1)S(1)} %get-tuple-element.32), channel_id=1, source_target_pairs={{4,0},{8,4},{12,8},{16,12},{20,16},{24,20},{28,24},{5,1},{9,5},{13... | collective-permute-start | bytes 196616 | tf_op jit(solution)/shard_map/ppermute | solution.py:18
  111.8 6.5 %collective-permute-start.5 = (bf16[4,1,1024]{2,1,0:T(2,128)(2,1)S(1)}, bf16[4,1,1024]{2,1,0:T(2,128)(2,1)S(1)}, u32[]{:S(2)}, u32[]{:S(2)}) collective-permute-start(bf16[4,1,1024]{2,1,0:T(2,128)(2,1)S(1)} %get-tuple-element.20), channel_id=1, source_target_pairs={{0,1},{1,2},{2,3},{4,5},{5,6},{6,7},{8,9},{9,10},{10,11},{12,13},{... | collective-permute-start | bytes 24584 | tf_op jit(solution)/shard_map/ppermute | solution.py:17
  116.2 4.5 %collective-permute-start.6 = (bf16[4,1,1024]{2,1,0:T(2,128)(2,1)S(1)}, bf16[4,1,1024]{2,1,0:T(2,128)(2,1)S(1)}, u32[]{:S(2)}, u32[]{:S(2)}) collective-permute-start(bf16[4,1,1024]{2,1,0:T(2,128)(2,1)S(1)} %get-tuple-element.28), channel_id=1, source_target_pairs={{1,0},{2,1},{3,2},{5,4},{6,5},{7,6},{9,8},{10,9},{11,10},{13,12},{... | collective-permute-start | bytes 24584 | tf_op jit(solution)/shard_map/ppermute | solution.py:18
Sparse Core Ops, SparseCore 0:
  21.6 28.4 all-gather.4
  52.0 23.5 all-gather.6
  82.5 17.3 reduce-scatter.1
